TPU v7x, 32 devices: a whole 2x2x4 slice. The times are simulated.
32 devices in a mesh: groups: 2 (over y), segment: 4 (over z), dp: 4 (over x, core).
Axes of the slice: x: 2, y: 2, z: 4, core: 2. Of those that a mesh axis runs over, the one named last changes fastest.
Arguments:
- layer_input: bfloat16 [16, 4, 32, 2560], P('groups', 'dp'), parts along dimension 0, may hold values from -6 to 6
- attn_gain: float32 [4, 2560], P('segment'), may hold values from 0.5 to 1.5
- qkv_weight: bfloat16 [4, 2560, 3584], P('segment', 'dp')
- final_gain: float32 [2560], replicated, may hold values from 0.5 to 1.5
- head_weight: bfloat16 [2560, 10240], P('dp', 'segment')
- vocab_blocks: int32 [16, 2, 4], P('groups'), parts along dimension 0, may hold values from 0 to 79, as said below
- languages: int32 [16, 4, 32], P('groups', 'dp'), parts along dimension 0, may hold values from 0 to 1
- targets: int32 [16, 4, 32], P('groups', 'dp'), parts along dimension 0, may hold values from 0 to 511
- teacher: bfloat16 [16, 4, 32, 512], P('groups', 'dp'), parts along dimension 0, may hold values from 1.9431114e-05 to 0.0078125
Outputs:
- kl_loss: float32 [16, 4, 32], P('groups', 'dp'), parts along dimension 0
- ce_loss: float32 [16, 4, 32], P('groups', 'dp'), parts along dimension 0
There are 2 independent parts, one for each index of `groups`. A program takes and returns all parts, laid end to end along the dimension named above; an argument that names none is the same for every part. Nothing has to cross between parts.
Inputs may be any that keep to these rules, and one draw needn't show every extreme that they name: `vocab_blocks`: each list names 4 different blocks. Section s holds blocks s * 20 to (s + 1) * 20 - 1; at most 2 blocks of one list lie in one section, and for every list some section holds exactly 2.
All inputs are finite; a program needn't handle non-finite values.
Results may differ from a plain program's by a relative error of at most 0.01.
Values may be sent and summed in bfloat16 or wider, within the bound.
No kernel may reach another device: no remote copies, remote signals or barrier semaphores. Data moves between devices by JAX's collectives and lax.ppermute only.
A program may use at most 128 MiB of HBM per device.

v0:
```python
import jax
import jax.numpy as jnp
from jax import lax
from jax.sharding import PartitionSpec as P

HEAD = 128
QHEADS = 20
KVHEADS = 4
BLOCK = 128
VB_SEGMENT = 20
CAP = 2


EPSILON = 1e-06
NEG_FILL = -1e30


def passed_along(value, axis, steps):
    count = lax.axis_size(axis)
    first, last = (max(0, -steps), min(count, count - steps))
    return lax.ppermute(value, axis, [(source, source + steps) for source in range(first, last)])


def from_root(value, axis, source):
    kept = jnp.where(lax.axis_index(axis) == source, value, 0).astype(value.dtype)
    return lax.psum(kept, axis)


def joined(part, axis, combine):
    gathered = jax.tree.map(lambda a: lax.all_gather(a, axis), part)

    def take(source):
        return jax.tree.map(lambda a: lax.dynamic_index_in_dim(a, source, 0, False), gathered)

    return lax.fori_loop(
        1, lax.axis_size(axis), lambda source, state: combine(state, take(source)), take(0)
    )


def rms_scaled(values, norm_gain):
    mean_sq = jnp.mean(values * values, axis=-1, keepdims=True)
    return values * lax.rsqrt(mean_sq + EPSILON) * norm_gain


def section(residual, norm_gain, weight):
    batch_size, length, feature_width = residual.shape
    widened = residual.astype(jnp.float32)
    normed = rms_scaled(widened, norm_gain).astype(jnp.bfloat16)
    projected = jnp.dot(
        normed.reshape(batch_size * length, feature_width),
        weight,
        preferred_element_type=jnp.float32,
    )
    projected = projected.astype(jnp.bfloat16).reshape(batch_size, length, -1)
    groups = QHEADS // KVHEADS
    queries = projected[:, :, : QHEADS * HEAD].reshape(batch_size, length, KVHEADS, groups, HEAD)
    key_rows = projected[:, :, QHEADS * HEAD : QHEADS * HEAD + KVHEADS * HEAD].reshape(
        batch_size, length, KVHEADS, HEAD
    )
    value_rows = projected[:, :, QHEADS * HEAD + KVHEADS * HEAD :].reshape(
        batch_size, length, KVHEADS, HEAD
    )
    scores = jnp.einsum(
        "bqhgd,bkhd->bhgqk", queries, key_rows, preferred_element_type=jnp.float32
    ) * HEAD ** (-0.5)
    positions = jnp.arange(length, dtype=jnp.int32)
    causal = positions[:, None] >= positions[None, :]
    scores = jnp.where(causal, scores, NEG_FILL)
    row_max = jnp.max(scores, axis=-1, keepdims=True)
    expanded = jnp.exp(scores - row_max)
    weights = (expanded / jnp.sum(expanded, axis=-1, keepdims=True)).astype(jnp.bfloat16)
    attended = jnp.einsum(
        "bhgqk,bkhd->bqhgd", weights, value_rows, preferred_element_type=jnp.float32
    )
    attended = attended.reshape(batch_size, length, QHEADS * HEAD)
    return (widened + attended).astype(jnp.bfloat16)


def softmax_pair(first, second):
    row_max = jnp.maximum(first[0], second[0])
    return (
        row_max,
        first[1] * jnp.exp(first[0] - row_max) + second[1] * jnp.exp(second[0] - row_max),
    )


def on_device(
    layer_input,
    attn_gain,
    qkv_weight,
    final_gain,
    head_weight,
    vocab_blocks,
    languages,
    targets,
    teacher,
):
    segment_idx = lax.axis_index("segment")
    segment_count = lax.axis_size("segment")
    batches = layer_input.shape[0]
    length = layer_input.shape[2]
    feature_width = layer_input.shape[3]
    layer_weight = lax.all_gather(qkv_weight[0], "dp", axis=0, tiled=True)
    layer_gain = attn_gain[0]
    sequences = layer_input[:, 0]

    def turn(step_idx, loop_state):
        incoming, finished = loop_state
        batch_idx = step_idx - segment_idx
        active = (batch_idx >= 0) & (batch_idx < batches)
        clipped = jnp.clip(batch_idx, 0, batches - 1)
        fresh = lax.dynamic_index_in_dim(sequences, clipped, 0, keepdims=False)
        source = jnp.where(segment_idx == 0, fresh, incoming)
        result = lax.cond(
            active,
            lambda rows_in: section(rows_in[None], layer_gain, layer_weight)[0],
            lambda rows_in: rows_in,
            source,
        )
        placed = lax.dynamic_update_index_in_dim(finished, result, clipped, 0)
        finished = jnp.where(active & (segment_idx == segment_count - 1), placed, finished)
        passed = passed_along(result, "segment", 1)
        return (passed, finished)

    start_state = (
        jnp.zeros((length, feature_width), jnp.bfloat16),
        jnp.zeros((batches, length, feature_width), jnp.bfloat16),
    )
    _, finished = lax.fori_loop(0, batches + segment_count - 1, turn, start_state)
    last_layer = from_root(finished, "segment", segment_count - 1)
    hidden = rms_scaled(last_layer.astype(jnp.float32), final_gain).astype(jnp.bfloat16)
    lang_count = vocab_blocks.shape[1]
    list_len = vocab_blocks.shape[2]
    owned = vocab_blocks // VB_SEGMENT == segment_idx
    order = jnp.cumsum(owned.astype(jnp.int32), axis=-1) - 1
    slot_ids = jnp.arange(CAP, dtype=jnp.int32)
    slot_hit = owned[:, :, None, :] & (order[:, :, None, :] == slot_ids[None, None, :, None])
    slot_valid = jnp.any(slot_hit, axis=-1)
    slot_pos = jnp.sum(jnp.where(slot_hit, jnp.arange(list_len, dtype=jnp.int32), 0), axis=-1)
    slot_local = jnp.sum(jnp.where(slot_hit, vocab_blocks[:, :, None, :] % VB_SEGMENT, 0), axis=-1)
    slot_width = lang_count * CAP * BLOCK
    spread = lax.all_to_all(hidden[None], "dp", split_axis=3, concat_axis=0, tiled=True)
    replicas = spread.shape[0]
    own_rows = spread.reshape(replicas * batches * length, spread.shape[3])
    row_count = head_weight.shape[0]
    shaped = head_weight.reshape(row_count, VB_SEGMENT, BLOCK)
    chosen = jnp.take(shaped, slot_local.reshape(-1), axis=1)
    chosen_own = chosen.reshape(row_count, batches, slot_width)
    row_part = own_rows
    row_part = row_part.reshape(
        batches * length * lax.axis_size("dp") // (batches * length),
        batches,
        length,
        own_rows.shape[1],
    )
    partial_value = jnp.einsum(
        "rbsd,dbc->rbsc", row_part, chosen_own, preferred_element_type=jnp.float32
    )
    slot_logits = (
        lax.psum_scatter(
            partial_value.reshape(batches * length * lax.axis_size("dp"), slot_width).astype(
                jnp.bfloat16
            ),
            "dp",
            scatter_dimension=0,
            tiled=True,
        )
        .astype(jnp.float32)
        .reshape(batches, length, slot_width)
    )
    token_langs = languages[:, 0]
    lang_pick = token_langs[:, :, None] == jnp.arange(lang_count, dtype=jnp.int32)
    per_lang = slot_logits.reshape(batches, length, lang_count, CAP, BLOCK)
    logits = jnp.sum(jnp.where(lang_pick[..., None, None], per_lang, 0.0), axis=2)
    token_valid = jnp.any(lang_pick[..., None] & slot_valid[:, None, :, :], axis=2)
    token_pos = jnp.sum(jnp.where(lang_pick[..., None], slot_pos[:, None, :, :], 0), axis=2)
    probs_all = teacher[:, 0].reshape(batches, length, list_len, BLOCK)
    token_probs = jnp.take_along_axis(probs_all, token_pos[..., None], axis=2).astype(jnp.float32)
    valid_cells = token_valid[..., None]
    masked = jnp.where(valid_cells, logits, NEG_FILL)
    local_max = jnp.max(masked, axis=(2, 3))
    local_total = jnp.sum(
        jnp.where(valid_cells, jnp.exp(masked - local_max[..., None, None]), 0.0), axis=(2, 3)
    )
    local_cross = jnp.sum(jnp.where(valid_cells, token_probs * logits, 0.0), axis=(2, 3))
    target_block = targets[:, 0] // BLOCK
    target_col = targets[:, 0] % BLOCK
    target_hit = valid_cells & (token_pos[..., None] == target_block[:, :, None, None])
    target_hit = target_hit & (jnp.arange(BLOCK, dtype=jnp.int32) == target_col[:, :, None, None])
    local_target = jnp.sum(jnp.where(target_hit, logits, 0.0), axis=(2, 3))
    row_max, row_total = joined((local_max, local_total), "segment", softmax_pair)
    cross_sum, target_logit = lax.psum((local_cross, local_target), "segment")
    log_total = row_max + jnp.log(row_total)
    full_probs = teacher[:, 0].astype(jnp.float32)
    self_sum = jnp.sum(full_probs * jnp.log(full_probs), axis=-1)
    prob_sum = jnp.sum(full_probs, axis=-1)
    kl_loss = self_sum - cross_sum + prob_sum * log_total
    ce_loss = log_total - target_logit
    return (kl_loss[:, None], ce_loss[:, None])


def solution(mesh):
    return jax.shard_map(
        on_device,
        mesh=mesh,
        in_specs=(
            P("groups", "dp", None, None),
            P("segment", None),
            P("segment", "dp", None),
            P(),
            P("dp", "segment"),
            P("groups", None, None),
            P("groups", "dp", None),
            P("groups", "dp", None),
            P("groups", "dp", None, None),
        ),
        out_specs=(P("groups", "dp", None), P("groups", "dp", None)),
        check_vma=False,
    )
```

profile of v0, /device:TPU:0, one launch (start us, length us, event | category | flops | bytes accessed | tf_op | source)
XLA Modules:
  0.0 686.2 jit_solution(2451504794034345510)
XLA Ops:
  8.0 121.5 %all-gather.5.cloned.1.call-done = bf16[1,2560,3584]{2,1,0:T(8,128)(2,1)} async-done(((bf16[1,640,3584]{2,1,0:T(8,128)(2,1)}), bf16[1,2560,3584]{2,1,0:T(8,128)(2,1)}) %all-gather.5.cloned.1.call-update) | async-done | bytes 18350096 | tf_op jit(solution)/shard_map/all_gather | solution.py:103
  129.6 197.6 %while.33 = (s32[]{:T(128)}, bf16[32,2560]{1,0:T(8,128)(2,1)S(1)}, bf16[8,32,2560]{2,1,0:T(8,128)(2,1)S(1)}, s32[]{:T(128)}, pred[]{:T(512)}, /*index=5*/bf16[8,...) while((s32[]{:T(128)}, bf16[32,2560]{1,0:T(8,128)(2,1)S(1)}, ...), condition=%wide.region_13.14_spmd, body=%wide.region_7.13_spmd.sunk | while | flops 598949632 | bytes 24278292 | solution.py:129
  130.5 11.1 %conditional.2 = (bf16[32,2560]{1,0:T(8,128)(2,1)S(1)}) conditional(s32[]{:T(128)} %convert_element_type.116, bf16[32,2560]{1,0:T(8,128)(2,1)S(1)} %bitcast_select_fusion.4, (bf16[32,2560]{1,0:T(8,128)(2,1)S(1)}, f32[1,2560]{1,0:T(1,128)S(1)}, bf16[2560,3584]{1,0:T(8,128)(2,1)}) %tuple.103), branch_computations={%region_8.8_spmd, %region_9.12_spmd} | conditional | flops 598785792 | bytes 22639628 | solution.py:114
  130.8 9.5 %fusion.2 = bf16[1,32,3584]{2,1,0:T(8,128)(2,1)S(1)} fusion(bf16[2560,3584]{1,0:T(8,128)(2,1)} %get-tuple-element.297, bf16[32,2560]{1,0:T(8,128)(2,1)S(1)} %get-tuple-element.295, f32[2560]{0:T(1024)S(1)} %reduce.5, f32[32]{0:T(128)S(1)} %add_rsqrt_fusion), kind=kOutput, calls=%fused_computation.8 | convolution fusion | flops 587644928 | bytes 18753664 | tf_op jit(solution)/shard_map/while/body/eval_jaxpr/cond/branch_1_fun/dot_general | solution.py:49
  148.0 11.1 %conditional.2 = (bf16[32,2560]{1,0:T(8,128)(2,1)S(1)}) conditional(s32[]{:T(128)} %convert_element_type.116, bf16[32,2560]{1,0:T(8,128)(2,1)S(1)} %bitcast_select_fusion.4, (bf16[32,2560]{1,0:T(8,128)(2,1)S(1)}, f32[1,2560]{1,0:T(1,128)S(1)}, bf16[2560,3584]{1,0:T(8,128)(2,1)}) %tuple.103), branch_computations={%region_8.8_spmd, %region_9.12_spmd} | conditional | flops 598785792 | bytes 22639628 | solution.py:114
  148.3 9.5 %fusion.2 = bf16[1,32,3584]{2,1,0:T(8,128)(2,1)S(1)} fusion(bf16[2560,3584]{1,0:T(8,128)(2,1)} %get-tuple-element.297, bf16[32,2560]{1,0:T(8,128)(2,1)S(1)} %get-tuple-element.295, f32[2560]{0:T(1024)S(1)} %reduce.5, f32[32]{0:T(128)S(1)} %add_rsqrt_fusion), kind=kOutput, calls=%fused_computation.8 | convolution fusion | flops 587644928 | bytes 18753664 | tf_op jit(solution)/shard_map/while/body/eval_jaxpr/cond/branch_1_fun/dot_general | solution.py:49
  167.9 11.1 %conditional.2 = (bf16[32,2560]{1,0:T(8,128)(2,1)S(1)}) conditional(s32[]{:T(128)} %convert_element_type.116, bf16[32,2560]{1,0:T(8,128)(2,1)S(1)} %bitcast_select_fusion.4, (bf16[32,2560]{1,0:T(8,128)(2,1)S(1)}, f32[1,2560]{1,0:T(1,128)S(1)}, bf16[2560,3584]{1,0:T(8,128)(2,1)}) %tuple.103), branch_computations={%region_8.8_spmd, %region_9.12_spmd} | conditional | flops 598785792 | bytes 22639628 | solution.py:114
  168.1 9.5 %fusion.2 = bf16[1,32,3584]{2,1,0:T(8,128)(2,1)S(1)} fusion(bf16[2560,3584]{1,0:T(8,128)(2,1)} %get-tuple-element.297, bf16[32,2560]{1,0:T(8,128)(2,1)S(1)} %get-tuple-element.295, f32[2560]{0:T(1024)S(1)} %reduce.5, f32[32]{0:T(128)S(1)} %add_rsqrt_fusion), kind=kOutput, calls=%fused_computation.8 | convolution fusion | flops 587644928 | bytes 18753664 | tf_op jit(solution)/shard_map/while/body/eval_jaxpr/cond/branch_1_fun/dot_general | solution.py:49
  187.1 11.1 %conditional.2 = (bf16[32,2560]{1,0:T(8,128)(2,1)S(1)}) conditional(s32[]{:T(128)} %convert_element_type.116, bf16[32,2560]{1,0:T(8,128)(2,1)S(1)} %bitcast_select_fusion.4, (bf16[32,2560]{1,0:T(8,128)(2,1)S(1)}, f32[1,2560]{1,0:T(1,128)S(1)}, bf16[2560,3584]{1,0:T(8,128)(2,1)}) %tuple.103), branch_computations={%region_8.8_spmd, %region_9.12_spmd} | conditional | flops 598785792 | bytes 22639628 | solution.py:114
  187.4 9.5 %fusion.2 = bf16[1,32,3584]{2,1,0:T(8,128)(2,1)S(1)} fusion(bf16[2560,3584]{1,0:T(8,128)(2,1)} %get-tuple-element.297, bf16[32,2560]{1,0:T(8,128)(2,1)S(1)} %get-tuple-element.295, f32[2560]{0:T(1024)S(1)} %reduce.5, f32[32]{0:T(128)S(1)} %add_rsqrt_fusion), kind=kOutput, calls=%fused_computation.8 | convolution fusion | flops 587644928 | bytes 18753664 | tf_op jit(solution)/shard_map/while/body/eval_jaxpr/cond/branch_1_fun/dot_general | solution.py:49
  206.4 11.1 %conditional.2 = (bf16[32,2560]{1,0:T(8,128)(2,1)S(1)}) conditional(s32[]{:T(128)} %convert_element_type.116, bf16[32,2560]{1,0:T(8,128)(2,1)S(1)} %bitcast_select_fusion.4, (bf16[32,2560]{1,0:T(8,128)(2,1)S(1)}, f32[1,2560]{1,0:T(1,128)S(1)}, bf16[2560,3584]{1,0:T(8,128)(2,1)}) %tuple.103), branch_computations={%region_8.8_spmd, %region_9.12_spmd} | conditional | flops 598785792 | bytes 22639628 | solution.py:114
  206.6 9.5 %fusion.2 = bf16[1,32,3584]{2,1,0:T(8,128)(2,1)S(1)} fusion(bf16[2560,3584]{1,0:T(8,128)(2,1)} %get-tuple-element.297, bf16[32,2560]{1,0:T(8,128)(2,1)S(1)} %get-tuple-element.295, f32[2560]{0:T(1024)S(1)} %reduce.5, f32[32]{0:T(128)S(1)} %add_rsqrt_fusion), kind=kOutput, calls=%fused_computation.8 | convolution fusion | flops 587644928 | bytes 18753664 | tf_op jit(solution)/shard_map/while/body/eval_jaxpr/cond/branch_1_fun/dot_general | solution.py:49
  225.7 11.1 %conditional.2 = (bf16[32,2560]{1,0:T(8,128)(2,1)S(1)}) conditional(s32[]{:T(128)} %convert_element_type.116, bf16[32,2560]{1,0:T(8,128)(2,1)S(1)} %bitcast_select_fusion.4, (bf16[32,2560]{1,0:T(8,128)(2,1)S(1)}, f32[1,2560]{1,0:T(1,128)S(1)}, bf16[2560,3584]{1,0:T(8,128)(2,1)}) %tuple.103), branch_computations={%region_8.8_spmd, %region_9.12_spmd} | conditional | flops 598785792 | bytes 22639628 | solution.py:114
  225.9 9.5 %fusion.2 = bf16[1,32,3584]{2,1,0:T(8,128)(2,1)S(1)} fusion(bf16[2560,3584]{1,0:T(8,128)(2,1)} %get-tuple-element.297, bf16[32,2560]{1,0:T(8,128)(2,1)S(1)} %get-tuple-element.295, f32[2560]{0:T(1024)S(1)} %reduce.5, f32[32]{0:T(128)S(1)} %add_rsqrt_fusion), kind=kOutput, calls=%fused_computation.8 | convolution fusion | flops 587644928 | bytes 18753664 | tf_op jit(solution)/shard_map/while/body/eval_jaxpr/cond/branch_1_fun/dot_general | solution.py:49
  245.0 11.1 %conditional.2 = (bf16[32,2560]{1,0:T(8,128)(2,1)S(1)}) conditional(s32[]{:T(128)} %convert_element_type.116, bf16[32,2560]{1,0:T(8,128)(2,1)S(1)} %bitcast_select_fusion.4, (bf16[32,2560]{1,0:T(8,128)(2,1)S(1)}, f32[1,2560]{1,0:T(1,128)S(1)}, bf16[2560,3584]{1,0:T(8,128)(2,1)}) %tuple.103), branch_computations={%region_8.8_spmd, %region_9.12_spmd} | conditional | flops 598785792 | bytes 22639628 | solution.py:114
  245.2 9.5 %fusion.2 = bf16[1,32,3584]{2,1,0:T(8,128)(2,1)S(1)} fusion(bf16[2560,3584]{1,0:T(8,128)(2,1)} %get-tuple-element.297, bf16[32,2560]{1,0:T(8,128)(2,1)S(1)} %get-tuple-element.295, f32[2560]{0:T(1024)S(1)} %reduce.5, f32[32]{0:T(128)S(1)} %add_rsqrt_fusion), kind=kOutput, calls=%fused_computation.8 | convolution fusion | flops 587644928 | bytes 18753664 | tf_op jit(solution)/shard_map/while/body/eval_jaxpr/cond/branch_1_fun/dot_general | solution.py:49
  264.2 11.1 %conditional.2 = (bf16[32,2560]{1,0:T(8,128)(2,1)S(1)}) conditional(s32[]{:T(128)} %convert_element_type.116, bf16[32,2560]{1,0:T(8,128)(2,1)S(1)} %bitcast_select_fusion.4, (bf16[32,2560]{1,0:T(8,128)(2,1)S(1)}, f32[1,2560]{1,0:T(1,128)S(1)}, bf16[2560,3584]{1,0:T(8,128)(2,1)}) %tuple.103), branch_computations={%region_8.8_spmd, %region_9.12_spmd} | conditional | flops 598785792 | bytes 22639628 | solution.py:114
  264.5 9.5 %fusion.2 = bf16[1,32,3584]{2,1,0:T(8,128)(2,1)S(1)} fusion(bf16[2560,3584]{1,0:T(8,128)(2,1)} %get-tuple-element.297, bf16[32,2560]{1,0:T(8,128)(2,1)S(1)} %get-tuple-element.295, f32[2560]{0:T(1024)S(1)} %reduce.5, f32[32]{0:T(128)S(1)} %add_rsqrt_fusion), kind=kOutput, calls=%fused_computation.8 | convolution fusion | flops 587644928 | bytes 18753664 | tf_op jit(solution)/shard_map/while/body/eval_jaxpr/cond/branch_1_fun/dot_general | solution.py:49
  283.5 15.5 %collective-permute-start = (bf16[32,2560]{1,0:T(8,128)(2,1)S(1)}, bf16[32,2560]{1,0:T(8,128)(2,1)S(1)}, u32[]{:S(2)}, u32[]{:S(2)}) collective-permute-start(bf16[32,2560]{1,0:T(8,128)(2,1)S(1)} %get-tuple-element.545), channel_id=1, source_target_pairs={{0,4},{4,8},{8,12},{1,5},{5,9},{9,13},{2,6},{6,10},{10,14},{3,7},{... | collective-permute-start | bytes 491528 | tf_op jit(solution)/shard_map/while/body/eval_jaxpr/ppermute | solution.py:21
  311.0 13.3 %collective-permute-start = (bf16[32,2560]{1,0:T(8,128)(2,1)S(1)}, bf16[32,2560]{1,0:T(8,128)(2,1)S(1)}, u32[]{:S(2)}, u32[]{:S(2)}) collective-permute-start(bf16[32,2560]{1,0:T(8,128)(2,1)S(1)} %get-tuple-element.545), channel_id=1, source_target_pairs={{0,4},{4,8},{8,12},{1,5},{5,9},{9,13},{2,6},{6,10},{10,14},{3,7},{... | collective-permute-start | bytes 491528 | tf_op jit(solution)/shard_map/while/body/eval_jaxpr/ppermute | solution.py:21
  336.0 203.1 %all-reduce.3.cloned.1.call-done = bf16[8,32,2560]{1,0,2:T(8,128)(2,1)} async-done(((bf16[8,32,2560]{1,0,2:T(8,128)(2,1)}), bf16[8,32,2560]{1,0,2:T(8,128)(2,1)}) %all-reduce.3.cloned.1.call-update) | async-done | bytes 1310736 | tf_op jit(solution)/shard_map/psum | solution.py:26
  544.1 8.2 %fusion.50 = bf16[2560,1,8,32]{3,2,1,0:T(8,128)(2,1)} fusion(f32[2560]{0:T(1024)S(1)} %copy-done.5, f32[8,32]{1,0:T(8,128)S(1)} %add_rsqrt_fusion.1, bf16[8,32,2560]{1,0,2:T(8,128)(2,1)S(1)} %copy-done), kind=kLoop, calls=%fused_computation.103 | loop fusion | flops 2621440 | bytes 2632704
  552.3 7.5 %reshape.271 = bf16[4,2,81920]{2,1,0:T(2,128)(2,1)} reshape(bf16[2560,1,8,32]{3,2,1,0:T(8,128)(2,1)} %fusion.50) | data formatting | bytes 2621440
  575.6 7.8 %copy.64 = bf16[640,32,128]{0,2,1:T(8,128)(2,1)} copy(bf16[640,32,128]{2,0,1:T(8,128)(2,1)} %bitcast.102) | data formatting | bytes 10485760 | tf_op jit(solution)/shard_map/jit(_take)/gather | solution.py:147
  583.5 6.2 bitcast_select_fusion.2
  589.7 5.5 reshape.272
  595.2 5.7 copy.68
  611.6 19.0 %reduce-scatter.2.cloned.1.call-done = bf16[256,512]{1,0:T(8,128)(2,1)} async-done(((bf16[1024,512]{1,0:T(8,128)(2,1)}), bf16[256,512]{1,0:T(8,128)(2,1)}) %reduce-scatter.2.cloned.1.call-update) | async-done | bytes 262160 | tf_op jit(solution)/shard_map/reduce_scatter | solution.py:160
  633.6 13.2 %all-gather.1 = f32[32,32]{1,0:T(8,128)S(1)} all-gather(f32[8,32]{1,0:T(8,128)S(1)} %fusion.34), channel_id=3, replica_groups=mesh['groups'=2,'segment'=4,'dp'=4] {'segment'}, dimensions={0}, use_global_device_ids=true | all-gather | bytes 5120 | tf_op jit(solution)/shard_map/all_gather | solution.py:30
  646.8 7.2 %select_reduce_fusion.1 = (f32[8,32]{1,0:T(8,128)S(1)}, f32[8,32]{1,0:T(8,128)S(1)}, f32[8,32]{1,0:T(8,128)S(1)}) fusion(pred[8,32,2]{2,1,0:T(8,128)(4,1)S(1)} %copy.57, f32[8,32,2,128]{3,2,1,0:T(2,128)S(1)} %select_reduce_fusion, f32[8,32]{1,0:T(8,128)S(1)} %fusion.34, bf16[8,32,2,128]{3,2,1,0:T(2,128)(2,1)S(1)} %bitcast.108, ...), kind=kLoop, calls=%fused_computation.55 | loop fusion | flops 785664 | bytes 431616 | tf_op jit(solution)/shard_map/reduce_sum | solution.py:182
  654.0 13.2 %all-gather.2 = f32[32,32]{1,0:T(8,128)S(1)} all-gather(f32[8,32]{1,0:T(8,128)S(1)} %get-tuple-element.340), channel_id=4, replica_groups=mesh['groups'=2,'segment'=4,'dp'=4] {'segment'}, dimensions={0}, use_global_device_ids=true | all-gather | bytes 5120 | tf_op jit(solution)/shard_map/all_gather | solution.py:30
  667.3 11.8 %all-reduce = (f32[8,32]{1,0:T(8,128)S(1)}, f32[8,32]{1,0:T(8,128)S(1)}) all-reduce(f32[8,32]{1,0:T(8,128)S(1)} %get-tuple-element.341, f32[8,32]{1,0:T(8,128)S(1)} %get-tuple-element.342), channel_id=1, replica_groups=mesh['groups'=2,'segment'=4,'dp'=4] {'segment'}, use_global_device_ids=true, to_apply=%region_19.20 | all-reduce | flops 512 | bytes 4096 | tf_op jit(solution)/shard_map/psum | solution.py:192
  (238 shorter events, 136.3 us)
Async XLA Ops:
  7.2 122.4 %copy-start.3 = (f32[1,2560]{1,0:T(1,128)S(1)}, f32[1,2560]{1,0:T(1,128)}, u32[]{:S(2)}) copy-start(f32[1,2560]{1,0:T(1,128)} %param.16) | copy-start | bytes 30724
  7.2 122.3 %all-gather.5.cloned.1.call-start = ((), (), s32[]{:S(2)}) async-start(), calls=%async_computation.4 | async-start | bytes 22937600 | tf_op jit(solution)/shard_map/all_gather | solution.py:103
  7.9 531.2 %all-reduce.3.cloned.1.call-start = ((), (), s32[]{:S(2)}) async-start(), calls=%async_computation.2 | async-start | bytes 10485760 | tf_op jit(solution)/shard_map/psum | solution.py:26
  141.7 5.4 collective-permute-start
  159.2 7.8 %collective-permute-start = (bf16[32,2560]{1,0:T(8,128)(2,1)S(1)}, bf16[32,2560]{1,0:T(8,128)(2,1)S(1)}, u32[]{:S(2)}, u32[]{:S(2)}) collective-permute-start(bf16[32,2560]{1,0:T(8,128)(2,1)S(1)} %get-tuple-element.545), channel_id=1, source_target_pairs={{0,4},{4,8},{8,12},{1,5},{5,9},{9,13},{2,6},{6,10},{10,14},{3,7},{... | collective-permute-start | bytes 491528 | tf_op jit(solution)/shard_map/while/body/eval_jaxpr/ppermute | solution.py:21
  179.0 7.2 %collective-permute-start = (bf16[32,2560]{1,0:T(8,128)(2,1)S(1)}, bf16[32,2560]{1,0:T(8,128)(2,1)S(1)}, u32[]{:S(2)}, u32[]{:S(2)}) collective-permute-start(bf16[32,2560]{1,0:T(8,128)(2,1)S(1)} %get-tuple-element.545), channel_id=1, source_target_pairs={{0,4},{4,8},{8,12},{1,5},{5,9},{9,13},{2,6},{6,10},{10,14},{3,7},{... | collective-permute-start | bytes 491528 | tf_op jit(solution)/shard_map/while/body/eval_jaxpr/ppermute | solution.py:21
  198.3 7.2 %collective-permute-start = (bf16[32,2560]{1,0:T(8,128)(2,1)S(1)}, bf16[32,2560]{1,0:T(8,128)(2,1)S(1)}, u32[]{:S(2)}, u32[]{:S(2)}) collective-permute-start(bf16[32,2560]{1,0:T(8,128)(2,1)S(1)} %get-tuple-element.545), channel_id=1, source_target_pairs={{0,4},{4,8},{8,12},{1,5},{5,9},{9,13},{2,6},{6,10},{10,14},{3,7},{... | collective-permute-start | bytes 491528 | tf_op jit(solution)/shard_map/while/body/eval_jaxpr/ppermute | solution.py:21
  217.5 7.2 %collective-permute-start = (bf16[32,2560]{1,0:T(8,128)(2,1)S(1)}, bf16[32,2560]{1,0:T(8,128)(2,1)S(1)}, u32[]{:S(2)}, u32[]{:S(2)}) collective-permute-start(bf16[32,2560]{1,0:T(8,128)(2,1)S(1)} %get-tuple-element.545), channel_id=1, source_target_pairs={{0,4},{4,8},{8,12},{1,5},{5,9},{9,13},{2,6},{6,10},{10,14},{3,7},{... | collective-permute-start | bytes 491528 | tf_op jit(solution)/shard_map/while/body/eval_jaxpr/ppermute | solution.py:21
  236.8 7.2 %collective-permute-start = (bf16[32,2560]{1,0:T(8,128)(2,1)S(1)}, bf16[32,2560]{1,0:T(8,128)(2,1)S(1)}, u32[]{:S(2)}, u32[]{:S(2)}) collective-permute-start(bf16[32,2560]{1,0:T(8,128)(2,1)S(1)} %get-tuple-element.545), channel_id=1, source_target_pairs={{0,4},{4,8},{8,12},{1,5},{5,9},{9,13},{2,6},{6,10},{10,14},{3,7},{... | collective-permute-start | bytes 491528 | tf_op jit(solution)/shard_map/while/body/eval_jaxpr/ppermute | solution.py:21
  256.1 7.2 %collective-permute-start = (bf16[32,2560]{1,0:T(8,128)(2,1)S(1)}, bf16[32,2560]{1,0:T(8,128)(2,1)S(1)}, u32[]{:S(2)}, u32[]{:S(2)}) collective-permute-start(bf16[32,2560]{1,0:T(8,128)(2,1)S(1)} %get-tuple-element.545), channel_id=1, source_target_pairs={{0,4},{4,8},{8,12},{1,5},{5,9},{9,13},{2,6},{6,10},{10,14},{3,7},{... | collective-permute-start | bytes 491528 | tf_op jit(solution)/shard_map/while/body/eval_jaxpr/ppermute | solution.py:21
  275.4 7.2 %collective-permute-start = (bf16[32,2560]{1,0:T(8,128)(2,1)S(1)}, bf16[32,2560]{1,0:T(8,128)(2,1)S(1)}, u32[]{:S(2)}, u32[]{:S(2)}) collective-permute-start(bf16[32,2560]{1,0:T(8,128)(2,1)S(1)} %get-tuple-element.545), channel_id=1, source_target_pairs={{0,4},{4,8},{8,12},{1,5},{5,9},{9,13},{2,6},{6,10},{10,14},{3,7},{... | collective-permute-start | bytes 491528 | tf_op jit(solution)/shard_map/while/body/eval_jaxpr/ppermute | solution.py:21
  283.5 18.3 %collective-permute-start = (bf16[32,2560]{1,0:T(8,128)(2,1)S(1)}, bf16[32,2560]{1,0:T(8,128)(2,1)S(1)}, u32[]{:S(2)}, u32[]{:S(2)}) collective-permute-start(bf16[32,2560]{1,0:T(8,128)(2,1)S(1)} %get-tuple-element.545), channel_id=1, source_target_pairs={{0,4},{4,8},{8,12},{1,5},{5,9},{9,13},{2,6},{6,10},{10,14},{3,7},{... | collective-permute-start | bytes 491528 | tf_op jit(solution)/shard_map/while/body/eval_jaxpr/ppermute | solution.py:21
  302.8 7.2 %collective-permute-start = (bf16[32,2560]{1,0:T(8,128)(2,1)S(1)}, bf16[32,2560]{1,0:T(8,128)(2,1)S(1)}, u32[]{:S(2)}, u32[]{:S(2)}) collective-permute-start(bf16[32,2560]{1,0:T(8,128)(2,1)S(1)} %get-tuple-element.545), channel_id=1, source_target_pairs={{0,4},{4,8},{8,12},{1,5},{5,9},{9,13},{2,6},{6,10},{10,14},{3,7},{... | collective-permute-start | bytes 491528 | tf_op jit(solution)/shard_map/while/body/eval_jaxpr/ppermute | solution.py:21
  311.0 16.1 %collective-permute-start = (bf16[32,2560]{1,0:T(8,128)(2,1)S(1)}, bf16[32,2560]{1,0:T(8,128)(2,1)S(1)}, u32[]{:S(2)}, u32[]{:S(2)}) collective-permute-start(bf16[32,2560]{1,0:T(8,128)(2,1)S(1)} %get-tuple-element.545), channel_id=1, source_target_pairs={{0,4},{4,8},{8,12},{1,5},{5,9},{9,13},{2,6},{6,10},{10,14},{3,7},{... | collective-permute-start | bytes 491528 | tf_op jit(solution)/shard_map/while/body/eval_jaxpr/ppermute | solution.py:21
  335.0 0.7 copy-start.4
  335.0 209.0 %copy-start.5 = (f32[2560]{0:T(1024)S(1)}, f32[2560]{0:T(1024)}, u32[]{:S(2)}) copy-start(f32[2560]{0:T(1024)} %param.18) | copy-start | bytes 30724
  539.1 5.0 copy-start
  552.3 12.1 %copy-start.1 = (bf16[640,2560]{1,0:T(8,128)(2,1)S(1)}, bf16[640,2560]{1,0:T(8,128)(2,1)}, u32[]{:S(2)}) copy-start(bf16[640,2560]{1,0:T(8,128)(2,1)} %param.19) | copy-start | bytes 9830404
  559.8 29.9 %all-to-all-start = ((bf16[4,2,81920]{2,1,0:T(2,128)(2,1)}), bf16[4,2,81920]{2,1,0:T(2,128)(2,1)}, u32[]{:S(2)}, u32[]{:S(2)}) async-start(bf16[4,2,81920]{2,1,0:T(2,128)(2,1)} %reshape.271), calls=%async_computation | async-start | bytes 2621440 | tf_op jit(solution)/shard_map/all_to_all | solution.py:142
  564.1 66.5 %reduce-scatter.2.cloned.1.call-start = ((), (), s32[]{:S(2)}) async-start(), calls=%async_computation.3 | async-start | bytes 1310720 | tf_op jit(solution)/shard_map/reduce_scatter | solution.py:160
  600.9 5.4 copy-start.7
  600.9 5.9 copy-start.6
  600.9 6.6 copy-start.2
Sparse Core Ops, SparseCore 0:
  9.6 119.7 all-gather.4
  335.2 203.8 all-reduce.2
  606.5 24.1 reduce-scatter.1
where the time goes:
time: 688 us; the launch traced here: 686 us
  waiting for transfers between devices  376 us (55%)
  matrix products  85.4 us (12%)
  starting transfers between devices  69.9 us (10%)
  local copies, waits for them, and re-layouts  55.5 us (8%)
  other arithmetic  45.7 us (7%)
  blocking collectives  38.1 us (6%)
  between operations  14 us (2%)
    psum x1, waiting for transfers between devices, from_root(): return lax.psum(kept, axis)  203 us
    all_gather x1, waiting for transfers between devices, on_device(): layer_weight = lax.all_gather(qkv_weight[0], 'dp', axis=0, tiled=True)  121 us
    dot_general x8, matrix products, section(): jnp.dot(normed.reshape(batch_size * length, feature_width), weight, prefe...  76.2 us
    ppermute x11, starting transfers between devices, passed_along(): lax.ppermute(value, axis, [(source, source + steps) for source in range(f...  65.3 us
    ppermute x11, waiting for transfers between devices, passed_along(): lax.ppermute(value, axis, [(source, source + steps) for source in range(f...  32.1 us
    all_gather x2, blocking collectives, joined(): gathered = jax.tree.map(lambda a: lax.all_gather(a, axis), part)  26.3 us
    reduce_scatter x1, waiting for transfers between devices, on_device(): lax.psum_scatter(partial_value.reshape(batches * length * lax.axis_size('...  19 us
    unnamed x19, local copies, waits for them, and re-layouts  17.2 us
  transfers between devices with their start and end apart: 15, of which 14 were waited for; matrix products, arithmetic and copies ran while one was open for 5% of the time, Pallas kernels for 0%

commit v1 on v0

v1 whole, which is shorter than its diff:
```python
import functools
import jax
import jax.numpy as jnp
from jax import lax
from jax.experimental import pallas as pl
from jax.experimental.pallas import tpu as pltpu
from jax.sharding import PartitionSpec as P

HEAD = 128
QHEADS = 20
KVHEADS = 4
BLOCK = 128
VB_SEGMENT = 20
CAP = 2
GROUP = QHEADS // KVHEADS

EPSILON = 1e-06
NEG_FILL = -1e30

CHUNK = 2
HOP = 2
UNROLL_LIMIT = 32


def section_kernel(seq_len, first_ref, fresh_ref, incoming_ref, gain_ref, wq_ref, wk_ref, wv_ref, out_ref, normed_ref):
    g = pl.program_id(0)
    is_first = first_ref[0] == 1
    tokens = fresh_ref.shape[0]

    @pl.when(g == 0)
    def _():
        rows = jnp.where(is_first, fresh_ref[...].astype(jnp.float32), incoming_ref[...].astype(jnp.float32))
        mean_sq = jnp.mean(rows * rows, axis=-1, keepdims=True)
        normed_ref[...] = (rows * lax.rsqrt(mean_sq + EPSILON) * gain_ref[...]).astype(jnp.bfloat16)

    normed = normed_ref[...]
    q = jnp.dot(normed, wq_ref[...], preferred_element_type=jnp.float32).astype(jnp.bfloat16)
    k = jnp.dot(normed, wk_ref[...], preferred_element_type=jnp.float32).astype(jnp.bfloat16)
    v = jnp.dot(normed, wv_ref[...], preferred_element_type=jnp.float32).astype(jnp.bfloat16)
    stacked = jnp.concatenate([q[:, h * HEAD : (h + 1) * HEAD] for h in range(GROUP)], axis=0)
    scores = lax.dot_general(stacked, k, (((1,), (1,)), ((), ())), preferred_element_type=jnp.float32)
    scores = scores * HEAD ** (-0.5)
    row_at = lax.rem(lax.broadcasted_iota(jnp.int32, scores.shape, 0), tokens)
    col_at = lax.broadcasted_iota(jnp.int32, scores.shape, 1)
    seen = (row_at >= col_at) & (lax.div(row_at, seq_len) == lax.div(col_at, seq_len))
    scores = jnp.where(seen, scores, NEG_FILL)
    row_max = jnp.max(scores, axis=-1, keepdims=True)
    expanded = jnp.exp(scores - row_max)
    probs = (expanded / jnp.sum(expanded, axis=-1, keepdims=True)).astype(jnp.bfloat16)
    attended = jnp.dot(probs, v, preferred_element_type=jnp.float32)
    for h in range(GROUP):
        cols = pl.ds(pl.multiple_of(g * (GROUP * HEAD) + h * HEAD, HEAD), HEAD)
        held = jnp.where(
            is_first, fresh_ref[:, cols].astype(jnp.float32), incoming_ref[:, cols].astype(jnp.float32)
        )
        out_ref[:, h * HEAD : (h + 1) * HEAD] = (held + attended[h * tokens : (h + 1) * tokens]).astype(jnp.bfloat16)


def section(first, fresh, incoming, gain, weight, seq_len):
    tokens, width = fresh.shape
    qw = GROUP * HEAD
    whole = pl.BlockSpec((tokens, width), lambda g, f: (0, 0))
    return pl.pallas_call(
        functools.partial(section_kernel, seq_len),
        out_shape=jax.ShapeDtypeStruct((tokens, width), jnp.bfloat16),
        grid_spec=pltpu.PrefetchScalarGridSpec(
            num_scalar_prefetch=1,
            grid=(KVHEADS,),
            in_specs=[
                whole,
                whole,
                pl.BlockSpec((1, width), lambda g, f: (0, 0)),
                pl.BlockSpec((width, qw), lambda g, f: (0, g)),
                pl.BlockSpec((width, HEAD), lambda g, f: (0, QHEADS + g)),
                pl.BlockSpec((width, HEAD), lambda g, f: (0, QHEADS + KVHEADS + g)),
            ],
            out_specs=pl.BlockSpec((tokens, qw), lambda g, f: (0, g)),
            scratch_shapes=[pltpu.VMEM((tokens, width), jnp.bfloat16)],
        ),
        compiler_params=pltpu.CompilerParams(vmem_limit_bytes=30 * 1024 * 1024),
        cost_estimate=pl.CostEstimate(
            flops=2 * tokens * weight.shape[0] * weight.shape[1],
            bytes_accessed=weight.size * 2 + 3 * tokens * width * 2,
            transcendentals=0,
        ),
        name="section",
    )(first, fresh, incoming, gain, weight, weight, weight)


def head_kernel(
    sources, per_source, local_ref, pos_ref, valid_ref, at_ref, *refs
):
    rows_refs = refs[: sources]
    gain_ref, lang_ref, target_ref, teacher_ref = refs[sources : sources + 4]
    block_refs = refs[sources + 4 : -1]
    out_ref = refs[-1]
    m = pl.program_id(0)
    slots = len(block_refs)
    picked = rows_refs[0][0].astype(jnp.float32)
    for i in range(1, sources):
        picked = jnp.where(at_ref[0] == i, rows_refs[i][0].astype(jnp.float32), picked)
    mean_sq = jnp.mean(picked * picked, axis=-1, keepdims=True)
    hidden = (picked * lax.rsqrt(mean_sq + EPSILON) * gain_ref[...]).astype(jnp.bfloat16)
    lang = lang_ref[0]
    target = target_ref[0]
    every = [jnp.dot(hidden, block_refs[i][...], preferred_element_type=jnp.float32) for i in range(slots)]
    shape = every[0].shape
    lane = lax.broadcasted_iota(jnp.int32, shape, 1)
    langs = slots // CAP
    kept = []
    for c in range(CAP):
        logits = jnp.zeros(shape, jnp.float32)
        probs = jnp.zeros(shape, jnp.float32)
        valid = jnp.zeros(lang.shape, jnp.int32)
        pos = jnp.zeros(lang.shape, jnp.int32)
        for l in range(langs):
            at = m * slots + l * CAP + c
            here = lang == l
            slot_pos = pos_ref[at]
            cols = pl.ds(pl.multiple_of(slot_pos * BLOCK, BLOCK), BLOCK)
            logits = jnp.where(here, every[l * CAP + c], logits)
            probs = jnp.where(here, teacher_ref[0, :, cols].astype(jnp.float32), probs)
            valid = jnp.where(here, valid_ref[at], valid)
            pos = jnp.where(here, slot_pos, pos)
        kept.append((logits, probs, valid == 1, pos))
    row_max = functools.reduce(
        jnp.maximum,
        [jnp.max(jnp.where(v, x, NEG_FILL), axis=-1, keepdims=True) for x, _, v, _ in kept],
    )
    total = jnp.zeros_like(row_max)
    cross = jnp.zeros_like(row_max)
    hit_sum = jnp.zeros_like(row_max)
    for x, p, v, pos in kept:
        total += jnp.sum(jnp.where(v, jnp.exp(jnp.where(v, x, NEG_FILL) - row_max), 0.0), axis=-1, keepdims=True)
        cross += jnp.sum(jnp.where(v, p * x, 0.0), axis=-1, keepdims=True)
        hit = v & (pos * BLOCK + lane == target)
        hit_sum += jnp.sum(jnp.where(hit, x, 0.0), axis=-1, keepdims=True)
    teach = teacher_ref[0].astype(jnp.float32)
    self_sum = jnp.sum(teach * jnp.log(teach), axis=-1, keepdims=True)
    prob_sum = jnp.sum(teach, axis=-1, keepdims=True)
    packed = jnp.zeros(shape, jnp.float32)
    for i, value in enumerate((row_max, total, cross, hit_sum, self_sum, prob_sum)):
        packed = jnp.where(lane == i, value, packed)
    out_ref[0] = packed.T[:8]


def head_stats(at, candidates, final_gain, langs_col, targets_col, teacher, head, local, pos, valid):
    batches, length, width = candidates[0].shape
    slots = local.shape[0] // batches
    sources = len(candidates)

    def block_spec(i):
        return pl.BlockSpec((width, BLOCK), lambda m, lo, po, va, a: (0, lo[m * slots + i]))

    per_batch = lambda *tail: pl.BlockSpec((1,) + tail, lambda m, lo, po, va, a: (m, 0, 0))
    return pl.pallas_call(
        functools.partial(head_kernel, sources, batches),
        out_shape=jax.ShapeDtypeStruct((batches, 8, length), jnp.float32),
        grid_spec=pltpu.PrefetchScalarGridSpec(
            num_scalar_prefetch=4,
            grid=(batches,),
            in_specs=[per_batch(length, width) for _ in range(sources)]
            + [
                pl.BlockSpec((1, width), lambda m, lo, po, va, a: (0, 0)),
                per_batch(length, 1),
                per_batch(length, 1),
                per_batch(length, teacher.shape[-1]),
            ]
            + [block_spec(i) for i in range(slots)],
            out_specs=per_batch(8, length),
        ),
        compiler_params=pltpu.CompilerParams(vmem_limit_bytes=30 * 1024 * 1024),
        cost_estimate=pl.CostEstimate(
            flops=2 * batches * length * width * slots * BLOCK,
            bytes_accessed=batches * width * slots * BLOCK * 2,
            transcendentals=0,
        ),
        name="head_stats",
    )(local, pos, valid, at, *candidates, final_gain, langs_col, targets_col, teacher, *([head] * slots))


def join_kernel(stats_ref, kl_ref, ce_ref):
    count = stats_ref.shape[0]
    stats = [stats_ref[s] for s in range(count)]
    row_max = functools.reduce(jnp.maximum, [s[:, 0, :] for s in stats])
    total = sum(s[:, 1, :] * jnp.exp(s[:, 0, :] - row_max) for s in stats)
    cross = sum(s[:, 2, :] for s in stats)
    hit = sum(s[:, 3, :] for s in stats)
    log_total = row_max + jnp.log(total)
    kl_ref[...] = stats[0][:, 4, :] - cross + stats[0][:, 5, :] * log_total
    ce_ref[...] = log_total - hit


def joined(stats):
    out = jax.ShapeDtypeStruct((stats.shape[1], stats.shape[3]), jnp.float32)
    return pl.pallas_call(join_kernel, out_shape=(out, out), name="join")(stats)


def shifted(value, axis, step, first, last):
    return lax.ppermute(value, axis, [(s, s + step) for s in range(first, last)])


def on_device(
    layer_input,
    attn_gain,
    qkv_weight,
    final_gain,
    head_weight,
    vocab_blocks,
    languages,
    targets,
    teacher,
):
    seg = lax.axis_index("segment")
    count = lax.axis_size("segment")
    batches, _, length, width = layer_input.shape
    chunk = CHUNK if batches % CHUNK == 0 else 1
    chunks = batches // chunk
    tokens = chunk * length
    weight = lax.all_gather(qkv_weight[0], "dp", axis=0, tiled=True)
    head_in, _ = lax.optimization_barrier((head_weight, weight))
    head = lax.all_gather(head_in, "dp", axis=0, tiled=True)
    fresh = layer_input.reshape(chunks, tokens, width)
    gain = attn_gain
    first = (seg == 0).astype(jnp.int32).reshape(1)

    langs = vocab_blocks.shape[1]
    list_len = vocab_blocks.shape[2]
    owned = vocab_blocks // VB_SEGMENT == seg
    order = jnp.cumsum(owned.astype(jnp.int32), axis=-1) - 1
    slot_ids = jnp.arange(CAP, dtype=jnp.int32)
    slot_hit = owned[:, :, None, :] & (order[:, :, None, :] == slot_ids[None, None, :, None])
    valid = jnp.any(slot_hit, axis=-1).astype(jnp.int32).reshape(-1)
    pos = jnp.sum(jnp.where(slot_hit, jnp.arange(list_len, dtype=jnp.int32), 0), axis=-1).reshape(-1)
    local = jnp.sum(jnp.where(slot_hit, vocab_blocks[:, :, None, :] % VB_SEGMENT, 0), axis=-1).reshape(-1)

    steps = chunks + HOP * (count - 1)
    zeros = jnp.zeros((tokens, width), jnp.bfloat16)
    if steps + count <= UNROLL_LIMIT:
        arrived = [zeros] * HOP
        results = []
        for t in range(steps):
            rows = section(first, fresh[min(t, chunks - 1)], arrived[t], gain, weight, length)
            results.append(rows)
            arrived.append(shifted(rows, "segment", 1, 0, count - 1) if t + HOP < steps else zeros)
        hops = [results[steps - chunks :]]
        for j in range(1, count):
            src = count - j
            hops.append([shifted(rows, "segment", -1, src, src + 1) for rows in hops[-1]])
        hops = [jnp.stack(h).reshape(batches, length, width) for h in hops]
        at = (count - 1 - seg).astype(jnp.int32).reshape(1)
    else:
        def turn(t, state):
            incoming, kept = state
            rows = section(first, fresh[jnp.minimum(t, chunks - 1)], incoming, gain, weight, length)
            kept = lax.dynamic_update_index_in_dim(kept, rows, jnp.clip(t - (count - 1), 0, chunks - 1), 0)
            return shifted(rows, "segment", 1, 0, count - 1), kept

        _, kept = lax.fori_loop(
            0, chunks + count - 1, turn, (zeros, jnp.zeros((chunks, tokens, width), jnp.bfloat16))
        )

        def back(j, value):
            moved = shifted(value, "segment", -1, 1, count)
            return jnp.where(seg == count - 1 - j, moved, value)

        kept = lax.fori_loop(1, count, back, kept)
        hops = [kept.reshape(batches, length, width)]
        at = jnp.zeros((1,), jnp.int32)
    stats = head_stats(
        at,
        hops,
        final_gain.reshape(1, width),
        languages.reshape(batches, length, 1),
        targets.reshape(batches, length, 1),
        teacher[:, 0],
        head,
        local,
        pos,
        valid,
    )
    kl, ce = joined(lax.all_gather(stats, "segment"))
    return kl[:, None], ce[:, None]


def solution(mesh):
    return jax.shard_map(
        on_device,
        mesh=mesh,
        in_specs=(
            P("groups", "dp", None, None),
            P("segment", None),
            P("segment", "dp", None),
            P(),
            P("dp", "segment"),
            P("groups", None, None),
            P("groups", "dp", None),
            P("groups", "dp", None),
            P("groups", "dp", None, None),
        ),
        out_specs=(P("groups", "dp", None), P("groups", "dp", None)),
        check_vma=False,
    )
```

time: 688 us -> 341 us (0.50)
  waiting for transfers between devices: 376 us -> 152 us
  Pallas kernels: 0 us -> 88.4 us
  matrix products: 85.4 us -> 0 us
  other arithmetic: 45.7 us -> 3.92 us
  starting transfers between devices: 69.9 us -> 30.7 us
  blocking collectives: 38.1 us -> 14.1 us
  local copies, waits for them, and re-layouts: 55.5 us -> 35.7 us
    psum x1 -> x0, waiting for transfers between devices: 203 us -> none  [from_root(): return lax.psum(kept, axis)]
    pallas_call x0 -> x12, Pallas kernels: none -> 88.4 us  [the longest x10 76.4 us: section(): pl.pallas_call(functools.partial(section_kernel, seq_len), out_shape=jax....]
    dot_general x25 -> x0, matrix products: 85.4 us -> none  [the longest x8 76.2 us: section(): jnp.dot(normed.reshape(batch_size * length, feature_width), weight, prefe...]
    ppermute x11 -> x20, starting transfers between devices: 65.3 us -> 30.6 us  [shifted(): lax.ppermute(value, axis, [(s, s + step) for s in range(first, last)])]
    select_n x26 -> x0, other arithmetic: 19.7 us -> none  [the longest x11 10.3 us: turn(): source = jnp.where(segment_idx == 0, fresh, incoming)]
    reduce_scatter x1 -> x0, waiting for transfers between devices: 19 us -> none  [on_device(): lax.psum_scatter(partial_value.reshape(batches * length * lax.axis_size('...]
    unnamed x19 -> x30, local copies, waits for them, and re-layouts: 17.2 us -> 34.8 us
    gather x5 -> x0, local copies, waits for them, and re-layouts: 15.3 us -> none  [the longest x2 11.4 us: on_device(): chosen = jnp.take(shaped, slot_local.reshape(-1), axis=1)]
  transfers between devices with their start and end apart: 15 -> 22, of which waited for: 14 -> 5; matrix products, arithmetic and copies ran while one was open for 5% -> 1% of each run, Pallas kernels for 0% -> 22%
where the time goes in v1:
time: 341 us; the launch traced here: 340 us
  waiting for transfers between devices  152 us (45%)
  Pallas kernels  88.4 us (26%)
  local copies, waits for them, and re-layouts  35.7 us (10%)
  starting transfers between devices  30.7 us (9%)
  between operations  14.6 us (4%)
  blocking collectives  14.1 us (4%)
  other arithmetic  3.92 us (1%)
    all_gather x1, waiting for transfers between devices, on_device(): weight = lax.all_gather(qkv_weight[0], 'dp', axis=0, tiled=True)  121 us
    pallas_call x10, Pallas kernels, section(): pl.pallas_call(functools.partial(section_kernel, seq_len), out_shape=jax....  76.4 us
    unnamed x30, local copies, waits for them, and re-layouts  34.8 us
    ppermute x20, starting transfers between devices, shifted(): lax.ppermute(value, axis, [(s, s + step) for s in range(first, last)])  30.6 us
    ppermute x20, waiting for transfers between devices, shifted(): lax.ppermute(value, axis, [(s, s + step) for s in range(first, last)])  30.1 us
    all_gather x1, blocking collectives, on_device(): kl, ce = joined(lax.all_gather(stats, 'segment'))  14.1 us
    pallas_call x1, Pallas kernels, head_stats(): pl.pallas_call(functools.partial(head_kernel, sources, batches), out_shap...  10.4 us
  transfers between devices with their start and end apart: 22, of which 5 were waited for; matrix products, arithmetic and copies ran while one was open for 1% of the time, Pallas kernels for 22%

profile of v1, /device:TPU:0, one launch (start us, length us, event | category | flops | bytes accessed | tf_op | source)
XLA Modules:
  0.0 339.6 jit_solution(14818850286325284781)
XLA Ops:
  7.9 121.5 %all-gather.7.cloned.1.call-done = bf16[1,2560,3584]{2,1,0:T(8,128)(2,1)} async-done(((bf16[1,640,3584]{2,1,0:T(8,128)(2,1)}), bf16[1,2560,3584]{2,1,0:T(8,128)(2,1)}) %all-gather.7.cloned.1.call-update) | async-done | bytes 18350096 | tf_op jit(solution)/shard_map/all_gather | solution.py:220
  131.4 6.6 %copy-done = bf16[1,2560,3584]{2,1,0:T(8,128)(2,1)S(1)} copy-done((bf16[1,2560,3584]{2,1,0:T(8,128)(2,1)S(1)}, bf16[1,2560,3584]{2,1,0:T(8,128)(2,1)}, u32[]{:S(2)}) %copy-start) | copy-done | bytes 18350104
  138.1 7.6 %section.14 = bf16[64,2560]{1,0:T(8,128)(2,1)S(1)} custom-call(s32[1]{0:T(128)} %bitcast.1.first_ref, bf16[64,2560]{1,0:T(8,128)(2,1)S(1)} %bitcast.84, bf16[64,2560]{1,0:T(8,128)(2,1)S(1)} %broadcast_in_dim.34.incoming_ref, f32[1,2560]{1,0:T(1,128)S(1)} %copy-done.7, bf16[2560,3584]{1,0:T(8,128)(2,1)S(1)} %bitcast.37, bf16[2560,3584]{1,0:T(8,128)(2,1)S(1)} %bitcast.38, ...), custom_call_target="tpu_custom_call" | custom-call | flops 1174405120 | bytes 19333120 | tf_op jit(solution)/shard_map/section/pallas_call | solution.py:63
  145.7 3.2 collective-permute-start.3
  148.9 6.3 %copy-done.1 = bf16[1,2560,3584]{2,1,0:T(8,128)(2,1)S(1)} copy-done((bf16[1,2560,3584]{2,1,0:T(8,128)(2,1)S(1)}, bf16[1,2560,3584]{2,1,0:T(8,128)(2,1)}, u32[]{:S(2)}) %copy-start.1) | copy-done | bytes 18350104
  155.3 7.6 %section.10 = bf16[64,2560]{1,0:T(8,128)(2,1)S(1)} custom-call(s32[1]{0:T(128)} %bitcast.1.first_ref, bf16[64,2560]{1,0:T(8,128)(2,1)S(1)} %bitcast.83, bf16[64,2560]{1,0:T(8,128)(2,1)S(1)} %broadcast_in_dim.34.incoming_ref, f32[1,2560]{1,0:T(1,128)S(1)} %copy-done.7, bf16[2560,3584]{1,0:T(8,128)(2,1)S(1)} %bitcast.40, bf16[2560,3584]{1,0:T(8,128)(2,1)S(1)} %bitcast.41, ...), custom_call_target="tpu_custom_call" | custom-call | flops 1174405120 | bytes 19333120 | tf_op jit(solution)/shard_map/section/pallas_call | solution.py:63
  162.9 3.4 %collective-permute-start = (bf16[64,2560]{1,0:T(8,128)(2,1)S(1)}, bf16[64,2560]{1,0:T(8,128)(2,1)S(1)}, u32[]{:S(2)}, u32[]{:S(2)}) collective-permute-start(bf16[64,2560]{1,0:T(8,128)(2,1)S(1)} %section.10), channel_id=1, source_target_pairs={{0,4},{4,8},{8,12},{1,5},{5,9},{9,13},{2,6},{6,10},{10,14},{3,7},{... | collective-permute-start | bytes 983048 | tf_op jit(solution)/shard_map/ppermute | solution.py:200
  166.4 6.4 %copy-done.2 = bf16[1,2560,3584]{2,1,0:T(8,128)(2,1)S(1)} copy-done((bf16[1,2560,3584]{2,1,0:T(8,128)(2,1)S(1)}, bf16[1,2560,3584]{2,1,0:T(8,128)(2,1)}, u32[]{:S(2)}) %copy-start.2) | copy-done | bytes 18350104
  172.8 7.6 %section.15 = bf16[64,2560]{1,0:T(8,128)(2,1)S(1)} custom-call(s32[1]{0:T(128)} %bitcast.1.first_ref, bf16[64,2560]{1,0:T(8,128)(2,1)S(1)} %bitcast.67, bf16[64,2560]{1,0:T(8,128)(2,1)S(1)} %collective-permute-done.3.incoming_ref, f32[1,2560]{1,0:T(1,128)S(1)} %copy-done.7, bf16[2560,3584]{1,0:T(8,128)(2,1)S(1)} %bitcast.43, ...), custom_call_target="tpu_custom_call" | custom-call | flops 1174405120 | bytes 19333120 | tf_op jit(solution)/shard_map/section/pallas_call | solution.py:63
  180.4 3.3 collective-permute-start.4
  183.8 7.7 %section.11 = bf16[64,2560]{1,0:T(8,128)(2,1)S(1)} custom-call(s32[1]{0:T(128)} %bitcast.1.first_ref, bf16[64,2560]{1,0:T(8,128)(2,1)S(1)} %bitcast.80, bf16[64,2560]{1,0:T(8,128)(2,1)S(1)} %collective-permute-done.incoming_ref, f32[1,2560]{1,0:T(1,128)S(1)} %copy-done.7, bf16[2560,3584]{1,0:T(8,128)(2,1)S(1)} %bitcast.46, bf16[2560,3584]{1,0:T(8,128)(2,1)S(1)} %bitcast.47, ...), custom_call_target="tpu_custom_call" | custom-call | flops 1174405120 | bytes 19333120 | tf_op jit(solution)/shard_map/section/pallas_call | solution.py:63
  191.4 1.9 collective-permute-start.1
  193.4 7.7 %section.16 = bf16[64,2560]{1,0:T(8,128)(2,1)S(1)} custom-call(s32[1]{0:T(128)} %bitcast.1.first_ref, bf16[64,2560]{1,0:T(8,128)(2,1)S(1)} %bitcast.68, bf16[64,2560]{1,0:T(8,128)(2,1)S(1)} %collective-permute-done.4.incoming_ref, f32[1,2560]{1,0:T(1,128)S(1)} %copy-done.7, bf16[2560,3584]{1,0:T(8,128)(2,1)S(1)} %bitcast.51, ...), custom_call_target="tpu_custom_call" | custom-call | flops 1174405120 | bytes 19333120 | tf_op jit(solution)/shard_map/section/pallas_call | solution.py:63
  201.0 2.1 collective-permute-start.5
  203.2 7.6 %section.12 = bf16[64,2560]{1,0:T(8,128)(2,1)S(1)} custom-call(s32[1]{0:T(128)} %bitcast.1.first_ref, bf16[64,2560]{1,0:T(8,128)(2,1)S(1)} %bitcast.69, bf16[64,2560]{1,0:T(8,128)(2,1)S(1)} %collective-permute-done.1.incoming_ref, f32[1,2560]{1,0:T(1,128)S(1)} %copy-done.7, bf16[2560,3584]{1,0:T(8,128)(2,1)S(1)} %bitcast.52, ...), custom_call_target="tpu_custom_call" | custom-call | flops 1174405120 | bytes 19333120 | tf_op jit(solution)/shard_map/section/pallas_call | solution.py:63
  210.8 1.9 collective-permute-start.2
  212.8 7.6 %section.17 = bf16[64,2560]{1,0:T(8,128)(2,1)S(1)} custom-call(s32[1]{0:T(128)} %bitcast.1.first_ref, bf16[64,2560]{1,0:T(8,128)(2,1)S(1)} %bitcast.70, bf16[64,2560]{1,0:T(8,128)(2,1)S(1)} %collective-permute-done.5.incoming_ref, f32[1,2560]{1,0:T(1,128)S(1)} %copy-done.7, bf16[2560,3584]{1,0:T(8,128)(2,1)S(1)} %bitcast.55, ...), custom_call_target="tpu_custom_call" | custom-call | flops 1174405120 | bytes 19333120 | tf_op jit(solution)/shard_map/section/pallas_call | solution.py:63
  220.5 2.1 collective-permute-start.7
  222.6 7.7 %section.13 = bf16[64,2560]{1,0:T(8,128)(2,1)S(1)} custom-call(s32[1]{0:T(128)} %bitcast.1.first_ref, bf16[64,2560]{1,0:T(8,128)(2,1)S(1)} %bitcast.71, bf16[64,2560]{1,0:T(8,128)(2,1)S(1)} %collective-permute-done.2.incoming_ref, f32[1,2560]{1,0:T(1,128)S(1)} %copy-done.7, bf16[2560,3584]{1,0:T(8,128)(2,1)S(1)} %bitcast.58, ...), custom_call_target="tpu_custom_call" | custom-call | flops 1174405120 | bytes 19333120 | tf_op jit(solution)/shard_map/section/pallas_call | solution.py:63
  230.3 1.9 collective-permute-start.6
  234.5 6.2 %copy-done.3 = bf16[1,2560,3584]{2,1,0:T(8,128)(2,1)S(1)} copy-done((bf16[1,2560,3584]{2,1,0:T(8,128)(2,1)S(1)}, bf16[1,2560,3584]{2,1,0:T(8,128)(2,1)}, u32[]{:S(2)}) %copy-start.3) | copy-done | bytes 18350104
  240.7 7.6 %section.19 = bf16[64,2560]{1,0:T(8,128)(2,1)S(1)} custom-call(s32[1]{0:T(128)} %bitcast.1.first_ref, bf16[64,2560]{1,0:T(8,128)(2,1)S(1)} %bitcast.72, bf16[64,2560]{1,0:T(8,128)(2,1)S(1)} %collective-permute-done.7.incoming_ref, f32[1,2560]{1,0:T(1,128)S(1)} %copy-done.7, bf16[2560,3584]{1,0:T(8,128)(2,1)S(1)} %bitcast.61, ...), custom_call_target="tpu_custom_call" | custom-call | flops 1174405120 | bytes 19333120 | tf_op jit(solution)/shard_map/section/pallas_call | solution.py:63
  249.0 7.7 %section.18 = bf16[64,2560]{1,0:T(8,128)(2,1)S(1)} custom-call(s32[1]{0:T(128)} %bitcast.1.first_ref, bf16[64,2560]{1,0:T(8,128)(2,1)S(1)} %bitcast.73, bf16[64,2560]{1,0:T(8,128)(2,1)S(1)} %collective-permute-done.6.incoming_ref, f32[1,2560]{1,0:T(1,128)S(1)} %copy-done.7, bf16[2560,3584]{1,0:T(8,128)(2,1)S(1)} %bitcast.64, ...), custom_call_target="tpu_custom_call" | custom-call | flops 1174405120 | bytes 19333120 | tf_op jit(solution)/shard_map/section/pallas_call | solution.py:63
  268.0 9.0 %collective-permute-done.17 = bf16[64,2560]{1,0:T(8,128)(2,1)S(1)} collective-permute-done((bf16[64,2560]{1,0:T(8,128)(2,1)S(1)}, bf16[64,2560]{1,0:T(8,128)(2,1)S(1)}, u32[]{:S(2)}, u32[]{:S(2)}) %collective-permute-start.17) | collective-permute-done | bytes 327712 | tf_op jit(solution)/shard_map/ppermute | solution.py:200
  277.0 7.0 %collective-permute-done.16 = bf16[64,2560]{1,0:T(8,128)(2,1)S(1)} collective-permute-done((bf16[64,2560]{1,0:T(8,128)(2,1)S(1)}, bf16[64,2560]{1,0:T(8,128)(2,1)S(1)}, u32[]{:S(2)}, u32[]{:S(2)}) %collective-permute-start.16) | collective-permute-done | bytes 327712 | tf_op jit(solution)/shard_map/ppermute | solution.py:200
  284.1 7.0 %collective-permute-done.19 = bf16[64,2560]{1,0:T(8,128)(2,1)S(1)} collective-permute-done((bf16[64,2560]{1,0:T(8,128)(2,1)S(1)}, bf16[64,2560]{1,0:T(8,128)(2,1)S(1)}, u32[]{:S(2)}, u32[]{:S(2)}) %collective-permute-start.19) | collective-permute-done | bytes 327712 | tf_op jit(solution)/shard_map/ppermute | solution.py:200
  291.1 7.0 %collective-permute-done.18 = bf16[64,2560]{1,0:T(8,128)(2,1)S(1)} collective-permute-done((bf16[64,2560]{1,0:T(8,128)(2,1)S(1)}, bf16[64,2560]{1,0:T(8,128)(2,1)S(1)}, u32[]{:S(2)}, u32[]{:S(2)}) %collective-permute-start.18) | collective-permute-done | bytes 327712 | tf_op jit(solution)/shard_map/ppermute | solution.py:200
  299.4 4.7 %copy-done.4 = bf16[2560,2560]{1,0:T(8,128)(2,1)S(1)} copy-done((bf16[2560,2560]{1,0:T(8,128)(2,1)S(1)}, bf16[2560,2560]{1,0:T(8,128)(2,1)}, u32[]{:S(2)}) %copy-start.4) | copy-done | bytes 13107224
  304.1 1.3 copy-done.5
  306.7 10.4 %head_stats.1 = f32[8,8,32]{2,1,0:T(8,128)S(1)} custom-call(s32[32]{0:T(128)S(1)} %reshape.67.local_ref, s32[32]{0:T(128)S(1)} %reshape.68.pos_ref, s32[32]{0:T(128)S(1)} %reshape.79.valid_ref, s32[1]{0:T(128)} %bitcast.at_ref, bf16[8,32,2560]{2,1,0:T(8,128)(2,1)S(1)} %bitcast.74, bf16[8,32,2560]{2,1,0:T(8,128)(2,1)S(1)} %bitcast.75, ...), custom_call_target="tpu_custom_call" | custom-call | flops 671088640 | bytes 20971520 | tf_op jit(solution)/shard_map/head_stats/pallas_call | solution.py:156
  317.1 14.1 %all-gather.1 = f32[32,8,32]{2,1,0:T(8,128)} all-gather(f32[8,8,32]{2,1,0:T(8,128)S(1)} %head_stats.1), channel_id=3, replica_groups=mesh['groups'=2,'segment'=4,'dp'=4] {'segment'}, dimensions={0}, use_global_device_ids=true | all-gather | bytes 40960 | tf_op jit(solution)/shard_map/all_gather | solution.py:282
  331.2 1.6 join.1
  (79 shorter events, 19.5 us)
Async XLA Ops:
  7.2 122.3 %all-gather.7.cloned.1.call-start = ((), (), s32[]{:S(2)}) async-start(), calls=%async_computation.1 | async-start | bytes 22937600 | tf_op jit(solution)/shard_map/all_gather | solution.py:220
  7.9 291.5 %all-gather.5.cloned.1.call-start = ((), (), s32[]{:S(2)}) async-start(), calls=%async_computation | async-start | bytes 16384000 | tf_op jit(solution)/shard_map/all_gather | solution.py:222
  131.4 6.6 %copy-start = (bf16[1,2560,3584]{2,1,0:T(8,128)(2,1)S(1)}, bf16[1,2560,3584]{2,1,0:T(8,128)(2,1)}, u32[]{:S(2)}) copy-start(bf16[1,2560,3584]{2,1,0:T(8,128)(2,1)} %all-gather.7.cloned.1.call-done) | copy-start | bytes 55050244
  145.7 20.7 %collective-permute-start.3 = (bf16[64,2560]{1,0:T(8,128)(2,1)S(1)}, bf16[64,2560]{1,0:T(8,128)(2,1)S(1)}, u32[]{:S(2)}, u32[]{:S(2)}) collective-permute-start(bf16[64,2560]{1,0:T(8,128)(2,1)S(1)} %section.14), channel_id=1, source_target_pairs={{0,4},{4,8},{8,12},{1,5},{5,9},{9,13},{2,6},{6,10},{10,14},{3,7},{... | collective-permute-start | bytes 983048 | tf_op jit(solution)/shard_map/ppermute | solution.py:200
  148.9 6.4 %copy-start.1 = (bf16[1,2560,3584]{2,1,0:T(8,128)(2,1)S(1)}, bf16[1,2560,3584]{2,1,0:T(8,128)(2,1)}, u32[]{:S(2)}) copy-start(bf16[1,2560,3584]{2,1,0:T(8,128)(2,1)} %all-gather.7.cloned.1.call-done) | copy-start | bytes 55050244
  155.3 11.1 %copy-start.11 = (s32[8,2,4]{0,2,1:T(4,128)S(1)}, s32[8,2,4]{0,2,1:T(4,128)}, u32[]{:S(2)}) copy-start(s32[8,2,4]{0,2,1:T(4,128)} %param.14) | copy-start | bytes 772
  162.9 20.8 %collective-permute-start = (bf16[64,2560]{1,0:T(8,128)(2,1)S(1)}, bf16[64,2560]{1,0:T(8,128)(2,1)S(1)}, u32[]{:S(2)}, u32[]{:S(2)}) collective-permute-start(bf16[64,2560]{1,0:T(8,128)(2,1)S(1)} %section.10), channel_id=1, source_target_pairs={{0,4},{4,8},{8,12},{1,5},{5,9},{9,13},{2,6},{6,10},{10,14},{3,7},{... | collective-permute-start | bytes 983048 | tf_op jit(solution)/shard_map/ppermute | solution.py:200
  166.4 6.4 %copy-start.2 = (bf16[1,2560,3584]{2,1,0:T(8,128)(2,1)S(1)}, bf16[1,2560,3584]{2,1,0:T(8,128)(2,1)}, u32[]{:S(2)}) copy-start(bf16[1,2560,3584]{2,1,0:T(8,128)(2,1)} %all-gather.7.cloned.1.call-done) | copy-start | bytes 55050244
  180.4 13.0 %collective-permute-start.4 = (bf16[64,2560]{1,0:T(8,128)(2,1)S(1)}, bf16[64,2560]{1,0:T(8,128)(2,1)S(1)}, u32[]{:S(2)}, u32[]{:S(2)}) collective-permute-start(bf16[64,2560]{1,0:T(8,128)(2,1)S(1)} %section.15), channel_id=1, source_target_pairs={{0,4},{4,8},{8,12},{1,5},{5,9},{9,13},{2,6},{6,10},{10,14},{3,7},{... | collective-permute-start | bytes 983048 | tf_op jit(solution)/shard_map/ppermute | solution.py:200
  191.4 11.7 %collective-permute-start.1 = (bf16[64,2560]{1,0:T(8,128)(2,1)S(1)}, bf16[64,2560]{1,0:T(8,128)(2,1)S(1)}, u32[]{:S(2)}, u32[]{:S(2)}) collective-permute-start(bf16[64,2560]{1,0:T(8,128)(2,1)S(1)} %section.11), channel_id=1, source_target_pairs={{0,4},{4,8},{8,12},{1,5},{5,9},{9,13},{2,6},{6,10},{10,14},{3,7},{... | collective-permute-start | bytes 983048 | tf_op jit(solution)/shard_map/ppermute | solution.py:200
  201.0 11.7 %collective-permute-start.5 = (bf16[64,2560]{1,0:T(8,128)(2,1)S(1)}, bf16[64,2560]{1,0:T(8,128)(2,1)S(1)}, u32[]{:S(2)}, u32[]{:S(2)}) collective-permute-start(bf16[64,2560]{1,0:T(8,128)(2,1)S(1)} %section.16), channel_id=1, source_target_pairs={{0,4},{4,8},{8,12},{1,5},{5,9},{9,13},{2,6},{6,10},{10,14},{3,7},{... | collective-permute-start | bytes 983048 | tf_op jit(solution)/shard_map/ppermute | solution.py:200
  210.8 11.8 %collective-permute-start.2 = (bf16[64,2560]{1,0:T(8,128)(2,1)S(1)}, bf16[64,2560]{1,0:T(8,128)(2,1)S(1)}, u32[]{:S(2)}, u32[]{:S(2)}) collective-permute-start(bf16[64,2560]{1,0:T(8,128)(2,1)S(1)} %section.12), channel_id=1, source_target_pairs={{0,4},{4,8},{8,12},{1,5},{5,9},{9,13},{2,6},{6,10},{10,14},{3,7},{... | collective-permute-start | bytes 983048 | tf_op jit(solution)/shard_map/ppermute | solution.py:200
  220.4 13.8 %copy-start.13 = (s32[8,1,32]{2,1,0:T(1,128)S(1)}, s32[8,1,32]{2,1,0:T(1,128)}, u32[]{:S(2)}) copy-start(s32[8,1,32]{2,1,0:T(1,128)} %param.15) | copy-start | bytes 3076
  220.4 13.9 %copy-start.14 = (s32[8,1,32]{2,1,0:T(1,128)S(1)}, s32[8,1,32]{2,1,0:T(1,128)}, u32[]{:S(2)}) copy-start(s32[8,1,32]{2,1,0:T(1,128)} %param.16) | copy-start | bytes 3076
  220.4 14.0 %copy-start.12 = (f32[2560]{0:T(1024)S(1)}, f32[2560]{0:T(1024)}, u32[]{:S(2)}) copy-start(f32[2560]{0:T(1024)} %param.12) | copy-start | bytes 30724
  220.5 14.0 %collective-permute-start.7 = (bf16[64,2560]{1,0:T(8,128)(2,1)S(1)}, bf16[64,2560]{1,0:T(8,128)(2,1)S(1)}, u32[]{:S(2)}, u32[]{:S(2)}) collective-permute-start(bf16[64,2560]{1,0:T(8,128)(2,1)S(1)} %section.17), channel_id=1, source_target_pairs={{0,4},{4,8},{8,12},{1,5},{5,9},{9,13},{2,6},{6,10},{10,14},{3,7},{... | collective-permute-start | bytes 983048 | tf_op jit(solution)/shard_map/ppermute | solution.py:200
  230.3 18.8 %collective-permute-start.6 = (bf16[64,2560]{1,0:T(8,128)(2,1)S(1)}, bf16[64,2560]{1,0:T(8,128)(2,1)S(1)}, u32[]{:S(2)}, u32[]{:S(2)}) collective-permute-start(bf16[64,2560]{1,0:T(8,128)(2,1)S(1)} %section.13), channel_id=1, source_target_pairs={{0,4},{4,8},{8,12},{1,5},{5,9},{9,13},{2,6},{6,10},{10,14},{3,7},{... | collective-permute-start | bytes 983048 | tf_op jit(solution)/shard_map/ppermute | solution.py:200
  232.2 25.2 %collective-permute-start.9 = (bf16[64,2560]{1,0:T(8,128)(2,1)S(1)}, bf16[64,2560]{1,0:T(8,128)(2,1)S(1)}, u32[]{:S(2)}, u32[]{:S(2)}) collective-permute-start(bf16[64,2560]{1,0:T(8,128)(2,1)S(1)} %section.17), channel_id=1, source_target_pairs={{12,8},{13,9},{14,10},{15,11},{28,24},{29,25},{30,26},{31,27}} | collective-permute-start | bytes 983048 | tf_op jit(solution)/shard_map/ppermute | solution.py:200
  232.9 25.2 %collective-permute-start.8 = (bf16[64,2560]{1,0:T(8,128)(2,1)S(1)}, bf16[64,2560]{1,0:T(8,128)(2,1)S(1)}, u32[]{:S(2)}, u32[]{:S(2)}) collective-permute-start(bf16[64,2560]{1,0:T(8,128)(2,1)S(1)} %section.13), channel_id=1, source_target_pairs={{12,8},{13,9},{14,10},{15,11},{28,24},{29,25},{30,26},{31,27}} | collective-permute-start | bytes 983048 | tf_op jit(solution)/shard_map/ppermute | solution.py:200
  234.5 6.2 %copy-start.3 = (bf16[1,2560,3584]{2,1,0:T(8,128)(2,1)S(1)}, bf16[1,2560,3584]{2,1,0:T(8,128)(2,1)}, u32[]{:S(2)}) copy-start(bf16[1,2560,3584]{2,1,0:T(8,128)(2,1)} %all-gather.7.cloned.1.call-done) | copy-start | bytes 55050244
  248.3 10.6 %collective-permute-start.11 = (bf16[64,2560]{1,0:T(8,128)(2,1)S(1)}, bf16[64,2560]{1,0:T(8,128)(2,1)S(1)}, u32[]{:S(2)}, u32[]{:S(2)}) collective-permute-start(bf16[64,2560]{1,0:T(8,128)(2,1)S(1)} %section.19), channel_id=1, source_target_pairs={{12,8},{13,9},{14,10},{15,11},{28,24},{29,25},{30,26},{31,27}} | collective-permute-start | bytes 983048 | tf_op jit(solution)/shard_map/ppermute | solution.py:200
  256.7 3.0 collective-permute-start.10
  257.4 3.0 collective-permute-start.13
  258.1 4.9 %copy-start.10 = (bf16[64,2560]{1,0:T(8,128)(2,1)}, bf16[64,2560]{1,0:T(8,128)(2,1)S(1)}, u32[]{:S(2)}) copy-start(bf16[64,2560]{1,0:T(8,128)(2,1)S(1)} %collective-permute-done.8) | copy-start | bytes 983044
  258.1 3.6 %collective-permute-start.12 = (bf16[64,2560]{1,0:T(8,128)(2,1)S(1)}, bf16[64,2560]{1,0:T(8,128)(2,1)S(1)}, u32[]{:S(2)}, u32[]{:S(2)}) collective-permute-start(bf16[64,2560]{1,0:T(8,128)(2,1)S(1)} %collective-permute-done.8), channel_id=1, source_target_pairs={{8,4},{9,5},{10,6},{11,7},{24,20},{25,21},{26,22},{27,23}} | collective-permute-start | bytes 983048 | tf_op jit(solution)/shard_map/ppermute | solution.py:200
  259.0 5.2 %collective-permute-start.15 = (bf16[64,2560]{1,0:T(8,128)(2,1)S(1)}, bf16[64,2560]{1,0:T(8,128)(2,1)S(1)}, u32[]{:S(2)}, u32[]{:S(2)}) collective-permute-start(bf16[64,2560]{1,0:T(8,128)(2,1)S(1)} %collective-permute-done.11), channel_id=1, source_target_pairs={{8,4},{9,5},{10,6},{11,7},{24,20},{25,21},{26,22},{27,23}} | collective-permute-start | bytes 983048 | tf_op jit(solution)/shard_map/ppermute | solution.py:200
  259.7 5.8 %collective-permute-start.14 = (bf16[64,2560]{1,0:T(8,128)(2,1)S(1)}, bf16[64,2560]{1,0:T(8,128)(2,1)S(1)}, u32[]{:S(2)}, u32[]{:S(2)}) collective-permute-start(bf16[64,2560]{1,0:T(8,128)(2,1)S(1)} %collective-permute-done.10), channel_id=1, source_target_pairs={{8,4},{9,5},{10,6},{11,7},{24,20},{25,21},{26,22},{27,23}} | collective-permute-start | bytes 983048 | tf_op jit(solution)/shard_map/ppermute | solution.py:200
  260.4 16.6 %collective-permute-start.17 = (bf16[64,2560]{1,0:T(8,128)(2,1)S(1)}, bf16[64,2560]{1,0:T(8,128)(2,1)S(1)}, u32[]{:S(2)}, u32[]{:S(2)}) collective-permute-start(bf16[64,2560]{1,0:T(8,128)(2,1)S(1)} %collective-permute-done.13), channel_id=1, source_target_pairs={{4,0},{5,1},{6,2},{7,3},{20,16},{21,17},{22,18},{23,19}} | collective-permute-start | bytes 983048 | tf_op jit(solution)/shard_map/ppermute | solution.py:200
  261.7 22.4 %collective-permute-start.16 = (bf16[64,2560]{1,0:T(8,128)(2,1)S(1)}, bf16[64,2560]{1,0:T(8,128)(2,1)S(1)}, u32[]{:S(2)}, u32[]{:S(2)}) collective-permute-start(bf16[64,2560]{1,0:T(8,128)(2,1)S(1)} %collective-permute-done.12), channel_id=1, source_target_pairs={{4,0},{5,1},{6,2},{7,3},{20,16},{21,17},{22,18},{23,19}} | collective-permute-start | bytes 983048 | tf_op jit(solution)/shard_map/ppermute | solution.py:200
  264.2 26.9 %collective-permute-start.19 = (bf16[64,2560]{1,0:T(8,128)(2,1)S(1)}, bf16[64,2560]{1,0:T(8,128)(2,1)S(1)}, u32[]{:S(2)}, u32[]{:S(2)}) collective-permute-start(bf16[64,2560]{1,0:T(8,128)(2,1)S(1)} %collective-permute-done.15), channel_id=1, source_target_pairs={{4,0},{5,1},{6,2},{7,3},{20,16},{21,17},{22,18},{23,19}} | collective-permute-start | bytes 983048 | tf_op jit(solution)/shard_map/ppermute | solution.py:200
  265.5 32.6 %collective-permute-start.18 = (bf16[64,2560]{1,0:T(8,128)(2,1)S(1)}, bf16[64,2560]{1,0:T(8,128)(2,1)S(1)}, u32[]{:S(2)}, u32[]{:S(2)}) collective-permute-start(bf16[64,2560]{1,0:T(8,128)(2,1)S(1)} %collective-permute-done.14), channel_id=1, source_target_pairs={{4,0},{5,1},{6,2},{7,3},{20,16},{21,17},{22,18},{23,19}} | collective-permute-start | bytes 983048 | tf_op jit(solution)/shard_map/ppermute | solution.py:200
  299.4 4.7 %copy-start.4 = (bf16[2560,2560]{1,0:T(8,128)(2,1)S(1)}, bf16[2560,2560]{1,0:T(8,128)(2,1)}, u32[]{:S(2)}) copy-start(bf16[2560,2560]{1,0:T(8,128)(2,1)} %all-gather.5.cloned.1.call-done.refs_8_.refs_9_.refs_10_.refs_11_) | copy-start | bytes 39321604
  (5 other events, 5.9 us)
Sparse Core Ops, SparseCore 0:
  9.6 119.7 all-gather.6
  131.0 85.0 all-gather.4
